TPU v7x, 512 devices: a whole 4x4x16 slice. The times are simulated.
512 devices in a mesh: grp: 4 (over z_hi, core), blk: 32 (over x, z_lo), tp: 4 (over y).
Axes of the slice: x: 4, y: 4, z: 16 (z_hi: 2, z_lo: 8; z = z_hi * 8 + z_lo), core: 2. Of those that a mesh axis runs over, the one named last changes fastest.
Arguments:
- hidden_in: bfloat16 [16384, 4096], P(('grp', 'blk')), may hold values from -24 to 24
- value_weight: bfloat16 [4096, 512], P('blk', 'tp'), may hold values from -0.09375 to 0.09375
- queries: bfloat16 [16384, 4096], P(('grp', 'blk'), 'tp'), may hold values from -30 to 30
- key_vectors: bfloat16 [16384, 512], P(('grp', 'blk'), 'tp'), may hold values from -6 to 6
- cotangent: bfloat16 [16384, 4096], P(('grp', 'blk'), 'tp'), may hold values from -0.0625 to 0.0625
- doc_ids: int32 [16384], P(('grp', 'blk')), may hold values from 0 to 4095, as said below
- positions: int32 [16384], P(('grp', 'blk')), may hold values from 0 to 4095, as said below
Outputs:
- attended: bfloat16 [16384, 4096], P(('grp', 'blk'), 'tp')
- value_grad: float32 [4096, 512], P(('grp', 'blk'), 'tp')
Inputs may be any that keep to these rules, and one draw needn't show every extreme that they name: `doc_ids`: the first group of 4096 tokens is one document; in every other group each document lies within the 128 tokens of one device, with ids unique within the group. Within a document positions count up from 0 in token order, except in the first group, where the devices' blocks of 128 positions follow an order given by a permutation of the devices.
All inputs are finite; a program needn't handle non-finite values.
Results may differ from a plain program's by a relative error of at most 0.017.
Values may be sent and summed in bfloat16 or wider, within the bound.
A program may use at most 64 MiB of HBM per device.

v0:
```python
import math

import jax
import jax.numpy as jnp
from jax import lax
from jax.sharding import PartitionSpec as P

HQ = 32
KVH = 4
HD = 128


def masked_scores(query_rows, key_block, query_docs, query_spots, key_docs, key_spots, score_scale):
    scores = (
        lax.dot_general(
            query_rows, key_block, (((1,), (1,)), ((), ())), preferred_element_type=jnp.float32
        )
        * score_scale
    )
    visible = (query_docs[:, None] == key_docs[None, :]) & (
        key_spots[None, :] <= query_spots[:, None]
    )
    return (scores, visible)


def block_split(seg_len):
    block_len = math.gcd(seg_len, 512)
    return (block_len, seg_len // block_len)


def attend_rows(
    query_rows,
    grad_rows,
    query_docs,
    query_spots,
    key_seg,
    value_seg,
    doc_seg,
    spot_seg,
    given_norm,
    score_scale,
):
    row_total = query_rows.shape[0]
    block_len, num_blocks = block_split(row_total)

    def advance(grad_total, pieces):
        q_blk, c_blk, d_blk, p_blk, n_blk = pieces
        scores, visible = masked_scores(
            q_blk, key_seg, d_blk, p_blk, doc_seg, spot_seg, score_scale
        )
        highest = jnp.max(jnp.where(visible, scores, -1e30), axis=1)
        norm_sum = jnp.sum(jnp.where(visible, jnp.exp(scores - highest[:, None]), 0.0), axis=1)
        log_norm = highest + jnp.log(norm_sum)
        weights = jnp.where(visible, jnp.exp(scores - log_norm[:, None]), 0.0).astype(jnp.bfloat16)
        out_blk = jnp.dot(weights, value_seg, preferred_element_type=jnp.float32).astype(
            jnp.bfloat16
        )
        grad_total = grad_total + lax.dot_general(
            weights, c_blk, (((0,), (0,)), ((), ())), preferred_element_type=jnp.float32
        )
        return (grad_total, out_blk)

    grad_total, outputs = lax.scan(
        advance,
        jnp.zeros((key_seg.shape[0], HD), jnp.float32),
        (
            query_rows.reshape(num_blocks, block_len, HD),
            grad_rows.reshape(num_blocks, block_len, HD),
            query_docs.reshape(num_blocks, block_len),
            query_spots.reshape(num_blocks, block_len),
            given_norm.reshape(num_blocks, block_len),
        ),
    )
    return (outputs.reshape(row_total, HD), grad_total)


def per_device(hidden_in, value_weight, queries, key_vectors, cotangent, doc_ids, positions):
    row_count = hidden_in.shape[0]
    group_size = HQ // KVH
    score_scale = HD ** (-0.5)
    columns = hidden_in
    projected = jnp.dot(
        columns,
        lax.all_gather(value_weight, "blk", axis=0, tiled=True),
        preferred_element_type=jnp.float32,
    )
    values = projected.astype(jnp.bfloat16)
    query_docs = jnp.repeat(doc_ids, group_size)
    query_spots = jnp.repeat(positions, group_size)
    span = group_size * HD
    query_rows = queries.reshape(row_count * group_size, HD)
    grad_rows = cotangent.reshape(row_count * group_size, HD)
    all_keys, all_values, all_docs, all_spots = (
        lax.all_gather(key_vectors, "blk", axis=0, tiled=True),
        lax.all_gather(values, "blk", axis=0, tiled=True),
        lax.all_gather(doc_ids, "blk", axis=0, tiled=True),
        lax.all_gather(positions, "blk", axis=0, tiled=True),
    )
    log_norms = jnp.zeros((row_count * group_size,), jnp.float32)
    out_head, grad_head = attend_rows(
        query_rows,
        grad_rows,
        query_docs,
        query_spots,
        all_keys,
        all_values,
        all_docs,
        all_spots,
        log_norms,
        score_scale,
    )
    outputs = out_head.reshape(row_count, span)
    value_grads = lax.psum_scatter(
        grad_head.astype(jnp.bfloat16), "blk", scatter_dimension=0, tiled=True
    )
    columns = hidden_in
    value_grad = lax.psum_scatter(
        lax.dot_general(
            columns, value_grads, (((0,), (0,)), ((), ())), preferred_element_type=jnp.float32
        ),
        ("grp", "blk"),
        scatter_dimension=0,
        tiled=True,
    )
    return (outputs, value_grad)


def solution(mesh):
    in_specs = (
        P(("grp", "blk"), None),
        P("blk", "tp"),
        P(("grp", "blk"), "tp"),
        P(("grp", "blk"), "tp"),
        P(("grp", "blk"), "tp"),
        P(("grp", "blk")),
        P(("grp", "blk")),
    )
    out_specs = (P(("grp", "blk"), "tp"), P(("grp", "blk"), "tp"))
    return jax.shard_map(
        per_device, mesh=mesh, in_specs=in_specs, out_specs=out_specs, check_vma=False
    )
```

profile of v0, /device:TPU:1, one launch (start us, length us, event | category | flops | bytes accessed | tf_op | source)
XLA Modules:
  0.0 1821.4 jit_solution(10809330940233549605)
XLA Ops:
  7.2 0.0 copy-start
  7.2 0.0 all-gather.8.cloned.1.call-start
  7.2 0.7 all-gather.8.cloned.1.call-update
  7.9 0.0 all-gather.6.cloned.1.call-start
  8.0 0.7 all-gather.6.cloned.1.call-update
  8.7 0.0 all-gather.10.cloned.1.call-start
  8.7 207.7 %all-gather.8.cloned.1.call-done = bf16[4096,128]{1,0:T(8,128)(2,1)} async-done(((bf16[128,128]{1,0:T(8,128)(2,1)}), bf16[4096,128]{1,0:T(8,128)(2,1)}) %all-gather.8.cloned.1.call-update) | async-done | bytes 1048592 | tf_op jit(solution)/shard_map/all_gather | solution.py:84
  216.4 0.0 copy-done
  216.4 2.3 convolution_convert_fusion.1
  218.6 0.0 all-gather.10.cloned.1.call-update
  218.7 0.0 reduce-scatter.5.cloned.1.call-start
  218.7 1.8 reshape_reshape.11
  220.5 1.1 reshape_reshape.12
  221.6 0.7 broadcast_in_dim.40
  222.3 0.1 broadcast_in_dim.41
  222.4 0.1 broadcast_in_dim.42
  222.5 0.7 broadcast_in_dim.43
  223.2 0.1 broadcast_in_dim.44
  223.3 0.1 broadcast_in_dim.45
  223.4 107.4 %all-gather = s32[32,1,128]{2,1,0:T(1,128)S(1)} all-gather(s32[1,1,128]{2,1,0:T(1,128)} %bitcast.55), channel_id=1, replica_groups=mesh['grp'=4,'blk'=32,'tp'=4] {'blk'}, dimensions={0}, use_global_device_ids=true | all-gather | bytes 16896 | tf_op jit(solution)/shard_map/all_gather | solution.py:96
  330.8 98.6 %all-gather.1 = s32[32,1,128]{2,1,0:T(1,128)S(1)} all-gather(s32[1,1,128]{2,1,0:T(1,128)} %bitcast.56), channel_id=1, replica_groups=mesh['grp'=4,'blk'=32,'tp'=4] {'blk'}, dimensions={0}, use_global_device_ids=true | all-gather | bytes 16896 | tf_op jit(solution)/shard_map/all_gather | solution.py:97
  429.5 9.2 all-gather.6.cloned.1.call-done
  438.6 223.4 %all-gather.10.cloned.1.call-done = bf16[4096,128]{1,0:T(8,128)(2,1)} async-done(((bf16[128,128]{1,0:T(8,128)(2,1)}), bf16[4096,128]{1,0:T(8,128)(2,1)}) %all-gather.10.cloned.1.call-update) | async-done | bytes 1048592 | tf_op jit(solution)/shard_map/all_gather | solution.py:95
  662.1 35.2 %while.13 = (s32[]{:T(128)}, f32[4096,128]{1,0:T(8,128)S(1)}, bf16[2,512,128]{2,1,0:T(8,128)(2,1)}, s32[2,512]{1,0:T(2,128)S(1)}, s32[4096]{0:T(1024)S(1)}, /*in...) while((s32[]{:T(128)}, f32[4096,128]{1,0:T(8,128)S(1)}, ...), condition=%wide.region_3.4_spmd.clone, body=%wide.region_0.3_spmd.clone.sunk | while | flops 1653669376 | bytes 65539268 | solution.py:63
  662.1 3.8 select_reduce_fusion.4
  665.9 3.1 select_reduce_fusion.5
  668.9 4.5 select_convert_fusion.2
  673.5 0.0 copy-start.1
  673.5 0.0 copy-start.2
  673.5 4.3 convolution_add_fusion.2
  677.7 0.0 copy-done.1
  677.7 0.0 copy-done.2
  677.7 1.9 fusion.28
  679.7 3.8 select_reduce_fusion.4
  683.5 3.1 select_reduce_fusion.5
  686.6 4.5 select_convert_fusion.2
  691.1 0.0 copy-start.1
  691.1 0.0 copy-start.2
  691.1 4.3 convolution_add_fusion.2
  695.3 0.0 copy-done.1
  695.3 0.0 copy-done.2
  695.4 1.9 fusion.28
  697.3 1.1 convert_element_type.13
  698.3 0.0 reduce-scatter.5.cloned.1.call-update
  698.4 0.0 reduce-scatter.7.cloned.1.call-start
  698.4 236.4 %reduce-scatter.5.cloned.1.call-done = bf16[128,128]{1,0:T(8,128)(2,1)} async-done(((bf16[4096,128]{1,0:T(8,128)(2,1)}), bf16[128,128]{1,0:T(8,128)(2,1)}) %reduce-scatter.5.cloned.1.call-update) | async-done | bytes 32784 | tf_op jit(solution)/shard_map/reduce_scatter | solution.py:113
  934.8 1.2 convolution_bitcast_fusion
  936.1 1.9 copy.12
  937.9 0.0 reduce-scatter.7.cloned.1.call-update
  937.9 1.8 reshape_reshape.13
  939.7 875.2 %reduce-scatter.7.cloned.1.call-done = f32[32,128]{1,0:T(8,128)} async-done(((f32[4096,128]{1,0:T(8,128)}), f32[32,128]{1,0:T(8,128)}) %reduce-scatter.7.cloned.1.call-update) | async-done | bytes 16400
  (6 shorter events, 0.0 us)
Async XLA Ops:
  7.2 209.2 %copy-start = (bf16[128,4096]{1,0:T(8,128)(2,1)S(1)}, bf16[128,4096]{1,0:T(8,128)(2,1)}, u32[]{:S(2)}) copy-start(bf16[128,4096]{1,0:T(8,128)(2,1)} %param.9) | copy-start | bytes 3145732
  7.2 209.2 %all-gather.8.cloned.1.call-start = ((), (), s32[]{:S(2)}) async-start(), calls=%async_computation.3 | async-start | bytes 1081344 | tf_op jit(solution)/shard_map/all_gather | solution.py:84
  7.9 430.7 %all-gather.6.cloned.1.call-start = ((), (), s32[]{:S(2)}) async-start(), calls=%async_computation.2 | async-start | bytes 1081344 | tf_op jit(solution)/shard_map/all_gather | solution.py:94
  8.7 653.4 %all-gather.10.cloned.1.call-start = ((), (), s32[]{:S(2)}) async-start(), calls=%async_computation.4 | async-start | bytes 1081344 | tf_op jit(solution)/shard_map/all_gather | solution.py:95
  218.7 716.2 %reduce-scatter.5.cloned.1.call-start = ((), (), s32[]{:S(2)}) async-start(), calls=%async_computation.5 | async-start | bytes 1081344 | tf_op jit(solution)/shard_map/reduce_scatter | solution.py:113
  673.5 4.3 copy-start.1
  673.5 4.3 copy-start.2
  691.1 4.3 copy-start.1
  691.1 4.3 copy-start.2
  698.4 1116.6 %reduce-scatter.7.cloned.1.call-start = ((), (), s32[]{:S(2)}) async-start(), calls=%async_computation.6 | async-start | bytes 2113536
Sparse Core Ops, SparseCore 0:
  10.1 206.2 all-gather.7
  218.5 220.1 all-gather.5
  440.7 221.2 all-gather.9
  698.5 236.3 reduce-scatter.4
  938.3 876.5 reduce-scatter.6
where the time goes:
time: 1820 us
  waiting for transfers between devices  1550 us (85%)
  blocking collectives  206 us (11%)
  matrix products  23.4 us (1%)
    unnamed x6, waiting for transfers between devices  877 us
    reduce_scatter x1, waiting for transfers between devices, per_device(): lax.psum_scatter(grad_head.astype(jnp.bfloat16), 'blk', scatter_dimension...  236 us
    all_gather x1, waiting for transfers between devices, per_device(): lax.all_gather(values, 'blk', axis=0, tiled=True)  223 us
    all_gather x1, waiting for transfers between devices, per_device(): lax.all_gather(value_weight, 'blk', axis=0, tiled=True)  208 us
    all_gather x1, blocking collectives, per_device(): lax.all_gather(doc_ids, 'blk', axis=0, tiled=True)  107 us
    all_gather x1, blocking collectives, per_device(): lax.all_gather(positions, 'blk', axis=0, tiled=True)  98.6 us
  transfers between devices with their start and end apart: 5, of which 5 were waited for; matrix products, arithmetic and copies ran while one was open for 0% of the time, Pallas kernels for 0%

commit v1 on v0

v1 whole, which is shorter than its diff:
```python
import functools
import math

import jax
import jax.numpy as jnp
from jax import lax
from jax.experimental import pallas as pl
from jax.experimental.pallas import tpu as pltpu
from jax.sharding import PartitionSpec as P

HD = 128
NX = 4
NZ = 8
TOK = 128
SCALE = HD ** (-0.5) * math.log2(math.e)
HIDDEN = -1e30
MESH = pl.DeviceIdType.MESH
BF = jnp.bfloat16
F32 = jnp.float32
NT = (((1,), (1,)), ((), ()))


def wait_for(ref, sem):
    pltpu.make_async_copy(ref, ref, sem).wait()


def flip(row, rows):
    return jnp.transpose(jnp.broadcast_to(row, (rows, row.shape[1])))


def stack_pair(block):
    return jnp.concatenate([block[:, :HD], block[:, HD:]], axis=0)


def kernel(
    hid, wgt, qry, key, cot, doc, pos,
    att, grad,
    posb, Ws, Hs, HsT, Kb, Kpos, KposT, Qb, Qpos, Cb, Qf, Cf, Sb, Pm, ML, Wr, Cs,
    Vp, Vr, Vb, VT, Tsend, Tsib, Tz, Tr, Vg, Ost, Or, Gst, Gr,
    ssem, rsem, lsem,
):
    grp = lax.axis_index("grp")
    blk = lax.axis_index("blk")
    tp = lax.axis_index("tp")
    zh, c = grp // 2, grp % 2
    x, z = blk // NZ, blk % NZ
    me = x * 2 + c
    z16 = zh * NZ + z
    trace = zh == 0
    not_trace = zh != 0
    main = jnp.logical_and(trace, c == 0)
    side = jnp.logical_and(trace, c == 1)
    local = jnp.logical_not(main)
    owner = jnp.where(trace, z // 4 == c, c == 0)
    trace_owner = jnp.logical_and(trace, z // 4 == c)
    w_self = jnp.logical_and(jnp.logical_and(c == x % 2, z // 2 == x), z % 2 == c)

    def dev(x_, z_, zh_, c_):
        return (zh_ * 2 + c_, x_ * NZ + z_, tp)

    def put(src, dst, phase, to):
        pltpu.make_async_remote_copy(
            src_ref=src, dst_ref=dst, send_sem=ssem.at[phase], recv_sem=rsem.at[phase],
            device_id=to, device_id_type=MESH,
        ).start()

    near = []
    for k in (1, 2, 7, 6, 3, 5, 4):
        s = (me + k) % 8
        near.append((s // 2, s % 2))
    sib = dev(x, z, zh, 1 - c)
    line = [(z + k) % NZ for k in (4, 3, 5, 2, 6, 1, 7)]

    bar = pltpu.get_barrier_semaphore()

    def greet(to):
        pl.semaphore_signal(bar, inc=1, device_id=to, device_id_type=MESH)

    for xs, cs in near:
        greet(dev(xs, z, zh, cs))
    for k in range(1, 16):
        zz = (z16 + k) % 16
        greet(dev(x, zz % NZ, zz // NZ, c))
    for gi in range(2):
        for j in range(2):
            xw = c + 2 * gi
            zw = 2 * x + j
            same = jnp.logical_and(w_self, jnp.logical_and(xw == x, zw == z))

            @pl.when(jnp.logical_not(same))
            def _():
                greet(dev(xw, zw, zh, z % 2))

    HQD = 512
    pltpu.make_async_copy(
        hid.at[:, pl.ds(pl.multiple_of(c * 1024 + x * 256, 256), 256)],
        Hs.at[me, :, pl.ds(0, 256)], lsem.at[0]).start()
    pltpu.make_async_copy(
        hid.at[:, pl.ds(pl.multiple_of((c + 2) * 1024 + x * 256, 256), 256)],
        Hs.at[me, :, pl.ds(256, 256)], lsem.at[1]).start()

    @pl.when(main)
    def _():
        pltpu.make_async_copy(qry.at[:, pl.ds(0, HQD)], Qb.at[x], lsem.at[2]).start()
        pltpu.make_async_copy(cot.at[:, pl.ds(0, HQD)], Cb.at[x], lsem.at[3]).start()

    @pl.when(local)
    def _():
        pltpu.make_async_copy(qry, Qf, lsem.at[4]).start()
        pltpu.make_async_copy(cot, Cf, lsem.at[5]).start()

    posb[...] = jnp.broadcast_to(pos[...], (8, TOK))

    @pl.when(main)
    def _():
        Kb[pl.ds(pl.multiple_of(z * TOK, TOK), TOK), :] = key[...]
        Kpos[z] = posb[...]
        Qpos[x] = posb[...]

    pl.semaphore_wait(bar, 22 + 4 - w_self.astype(jnp.int32))

    @pl.when(main)
    def _():
        for zz in line:
            put(key, Kb.at[pl.ds(pl.multiple_of(z * TOK, TOK), TOK), :], 0, dev(x, zz, zh, 0))
        for zz in line:
            put(posb, Kpos.at[z], 1, dev(x, zz, zh, 0))
        for xs, cs in near:
            to = dev(xs, z, zh, cs)
            put(qry.at[:, pl.ds(pl.multiple_of(cs * HQD, HQD), HQD)], Qb.at[x], 2, to)
            put(posb, Qpos.at[x], 3, to)

    slot = (x // 2) * 2 + z % 2
    for i in range(4):
        zt = 2 * i + c
        same = jnp.logical_and(w_self, zt == z)

        @pl.when(jnp.logical_not(same))
        def _():
            put(wgt, Ws.at[pl.ds(pl.multiple_of(slot * TOK, TOK), TOK), :], 4,
                dev(z // 2, zt, zh, x % 2))

    @pl.when(w_self)
    def _():
        pltpu.make_async_copy(
            wgt, Ws.at[pl.ds(pl.multiple_of(slot * TOK, TOK), TOK), :], rsem.at[4]).start()

    for xs, cs in near:
        to = dev(xs, z, zh, cs)
        for gi in range(2):
            col = pl.multiple_of((cs + 2 * gi) * 1024 + xs * 256, 256)
            put(hid.at[:, pl.ds(col, 256)], Hs.at[me, :, pl.ds(gi * 256, 256)], 5, to)

    @pl.when(main)
    def _():
        for xs, cs in near:
            put(cot.at[:, pl.ds(pl.multiple_of(cs * HQD, HQD), HQD)], Cb.at[x], 6,
                dev(xs, z, zh, cs))

    @pl.when(trace)
    def _():
        @pl.when(c == 0)
        def _():
            wait_for(Kb.at[pl.ds(0, 7 * TOK), :], rsem.at[0])
            put(Kb, Kb, 16, sib)
            wait_for(Kpos.at[pl.ds(0, 7)], rsem.at[1])
            put(Kpos, Kpos, 17, sib)
            wait_for(Qb.at[pl.ds(0, 3)], rsem.at[2])
            wait_for(Qpos.at[pl.ds(0, 3)], rsem.at[3])
            wait_for(Qb.at[0], lsem.at[2])

        @pl.when(c == 1)
        def _():
            wait_for(Kb, rsem.at[16])
            wait_for(Kpos, rsem.at[17])
            wait_for(Qb, rsem.at[2])
            wait_for(Qpos, rsem.at[3])

        for t in range(NZ):
            KposT[pl.ds(t * TOK, TOK), :] = flip(Kpos[t, 0:1, :].astype(F32), TOK)

        def score_block(xq, carry):
            q_at = Qpos[xq][0:1, :].astype(F32)
            tops, sums = [], []
            for pair in range(2):
                qp = stack_pair(Qb[xq, :, pl.ds(pair * 256, 256)])
                top = jnp.full((8, 256), HIDDEN, F32)
                for t in range(4):
                    rows = pl.ds(t * 256, 256)
                    s = lax.dot_general(Kb[rows, :], qp, NT, preferred_element_type=F32)
                    seen = KposT[rows, :] <= q_at
                    s = jnp.concatenate(
                        [jnp.where(seen, s[:, :HD], HIDDEN), jnp.where(seen, s[:, HD:], HIDDEN)],
                        axis=1)
                    Sb[rows, :] = s
                    top = jnp.maximum(top, jnp.max(s.reshape(32, 8, 256), axis=0))
                m = jnp.max(top, axis=0, keepdims=True) * SCALE
                total = jnp.zeros((8, 256), F32)
                at = pl.ds(pl.multiple_of(xq * 512 + pair * 256, 256), 256)
                for t in range(8):
                    rows = pl.ds(t * TOK, TOK)
                    p = jnp.exp2(Sb[rows, :] * SCALE - m)
                    total = total + jnp.sum(p.reshape(16, 8, 256), axis=0)
                    Pm[rows, at] = p.astype(BF)
                tops.append(m)
                sums.append(jnp.sum(total, axis=0, keepdims=True))
            ML[x, xq] = jnp.concatenate(
                tops + sums + [jnp.zeros((4, 256), F32)], axis=0)
            return carry

        lax.fori_loop(0, NX, score_block, 0)
        for k in (1, 3, 2):
            put(ML.at[x], ML.at[x], 7, dev((x + k) % NX, z, zh, c))

    wait_for(Ws, rsem.at[4])
    wait_for(Hs.at[pl.ds(0, 7)], rsem.at[5])
    wait_for(Hs.at[0, :, pl.ds(0, 256)], lsem.at[0])
    wait_for(Hs.at[0, :, pl.ds(0, 256)], lsem.at[1])

    def value_part(s, carry):
        Vp[s] = jnp.dot(Hs[s], Ws[...], preferred_element_type=F32).astype(BF)
        return carry

    lax.fori_loop(0, 8, value_part, 0)
    for xs, cs in near:
        put(Vp.at[xs * 2 + cs], Vr.at[me], 8, dev(xs, z, zh, cs))
    Vr[me] = Vp[me]
    for s in range(8):
        HsT[:, pl.ds(s * TOK, TOK)] = jnp.transpose(Hs[s])

    @pl.when(trace)
    def _():
        wait_for(ML.at[pl.ds(0, 3)], rsem.at[7])

        @pl.when(c == 0)
        def _():
            wait_for(Cb.at[pl.ds(0, 3)], rsem.at[6])
            wait_for(Cb.at[0], lsem.at[3])

        @pl.when(c == 1)
        def _():
            wait_for(Cb, rsem.at[6])

        def scale_block(xq, carry):
            parts = [ML[s, xq] for s in range(NX)]
            high = functools.reduce(jnp.maximum, [p[0:2] for p in parts])
            total = functools.reduce(
                jnp.add, [p[2:4] * jnp.exp2(p[0:2] - high) for p in parts])
            w = jnp.exp2(ML[x, xq][0:2] - high) / total
            Wr[xq] = jnp.concatenate([w, jnp.zeros((6, 256), F32)], axis=0)
            for pair in range(2):
                cp = stack_pair(Cb[xq, :, pl.ds(pair * 256, 256)]).astype(F32)
                rows = pl.ds(pl.multiple_of(xq * 512 + pair * 256, 256), 256)
                Cs[rows, :] = (cp * flip(w[pair:pair + 1], TOK)).astype(BF)
            return carry

        lax.fori_loop(0, NX, scale_block, 0)
        theirs = pl.ds(pl.multiple_of((1 - c) * 512, 512), 512)
        ours = pl.ds(pl.multiple_of(c * 512, 512), 512)
        Tsend[...] = jnp.dot(Pm[theirs, :], Cs[...], preferred_element_type=F32).astype(BF)
        put(Tsend, Tsib, 9, sib)
        mine = jnp.dot(Pm[ours, :], Cs[...], preferred_element_type=F32)
        wait_for(Tsib, rsem.at[9])
        Tz[...] = (mine + Tsib[...].astype(F32)).astype(BF).reshape(4, TOK, HD)
        for k in range(4):
            zt = 4 * c + k

            @pl.when(zt != z)
            def _():
                put(Tz.at[k], Tr.at[z], 10, dev(x, zt, zh, c))

            @pl.when(zt == z)
            def _():
                Tr[z] = Tz[k]

    wait_for(Vr.at[pl.ds(0, 7)], rsem.at[8])
    val = functools.reduce(jnp.add, [Vr[s].astype(F32) for s in range(8)]).astype(BF)

    @pl.when(main)
    def _():
        rows = pl.ds(pl.multiple_of(z * TOK, TOK), TOK)
        Vb[rows, :] = val
        for zz in line:
            put(Vb.at[rows, :], Vb.at[rows, :], 11, dev(x, zz, zh, 0))

    @pl.when(local)
    def _():
        wait_for(Qf, lsem.at[4])
        wait_for(Cf, lsem.at[5])
        val_t = jnp.transpose(val)
        p_row = pos[...].astype(F32)
        d_row = doc[...].astype(F32)
        seen = jnp.logical_and(flip(p_row, TOK) <= p_row, flip(d_row, TOK) == d_row)
        terms = jnp.zeros((TOK, HD), F32)
        for pair in range(4):
            qp = stack_pair(Qf[:, pl.ds(pair * 256, 256)])
            s = lax.dot_general(key[...], qp, NT, preferred_element_type=F32)
            s = jnp.concatenate(
                [jnp.where(seen, s[:, :HD], HIDDEN), jnp.where(seen, s[:, HD:], HIDDEN)], axis=1)
            s = s * SCALE
            p = jnp.exp2(s - jnp.max(s, axis=0, keepdims=True))
            w = 1.0 / jnp.sum(p, axis=0, keepdims=True)
            pb = (p * w).astype(BF)
            o = jnp.dot(val_t, pb, preferred_element_type=F32)
            att[:, pl.ds(pair * 256, HD)] = jnp.transpose(o[:, :HD]).astype(BF)
            att[:, pl.ds(pair * 256 + HD, HD)] = jnp.transpose(o[:, HD:]).astype(BF)
            cp = stack_pair(Cf[:, pl.ds(pair * 256, 256)])
            terms = terms + jnp.dot(pb, cp, preferred_element_type=F32)
        Vg[me] = terms.astype(BF)
        for phase, core in ((12, 0), (13, 1)):
            @pl.when(c == core)
            def _():
                for xs, cs in near:
                    put(Vg.at[me], Vg.at[me], phase, dev(xs, z, zh, cs))

    @pl.when(trace_owner)
    def _():
        wait_for(Tr.at[pl.ds(0, 7)], rsem.at[10])
        Vg[2 * x] = functools.reduce(
            jnp.add, [Tr[s].astype(F32) for s in range(NZ)]).astype(BF)
        for xs, cs in near:
            put(Vg.at[2 * x], Vg.at[2 * x], 12, dev(xs, z, zh, cs))

    for phase, sender in ((12, owner), (13, c == 1)):
        @pl.when(sender)
        def _():
            wait_for(Vg.at[pl.ds(0, 3)], rsem.at[phase])

        @pl.when(jnp.logical_not(sender))
        def _():
            wait_for(Vg.at[pl.ds(0, 4)], rsem.at[phase])

    vg_all = Vg[...].reshape(8 * TOK, HD)
    Gst[...] = jnp.dot(HsT[...], vg_all, preferred_element_type=F32).astype(BF).reshape(16, 32, HD)
    for k in (8, 7, 9, 6, 10, 5, 11, 4, 12, 3, 13, 2, 14, 1, 15):
        zz = (z16 + k) % 16
        put(Gst.at[zz], Gr.at[z16], 14, dev(x, zz % NZ, zz // NZ, c))
    Gr[z16] = Gst[z16]

    @pl.when(trace)
    def _():
        @pl.when(c == 0)
        def _():
            wait_for(Vb.at[pl.ds(0, 7 * TOK), :], rsem.at[11])
            put(Vb, Vb, 18, sib)

        @pl.when(c == 1)
        def _():
            wait_for(Vb, rsem.at[18])

        VT[...] = jnp.transpose(Vb[...])

        def out_block(xq, carry):
            w = Wr[xq]
            for pair in range(2):
                at = pl.ds(pl.multiple_of(xq * 512 + pair * 256, 256), 256)
                o = jnp.dot(VT[...], Pm[:, at], preferred_element_type=F32) * w[pair:pair + 1]
                Ost[xq, pl.ds(pair * 256, 256), :] = jnp.transpose(o).astype(BF)
            return carry

        lax.fori_loop(0, NX, out_block, 0)
        for k in range(NX):
            xt = (x + k) % NX
            if k == 0:
                @pl.when(c == 1)
                def _():
                    put(Ost.at[x], Or.at[me], 15, sib)

                @pl.when(c == 0)
                def _():
                    Or[me] = Ost[x]
            else:
                put(Ost.at[xt], Or.at[me], 15, dev(xt, z, zh, 0))

    @pl.when(main)
    def _():
        wait_for(Or.at[pl.ds(0, 7)], rsem.at[15])
        for half in range(2):
            for h in range(4):
                o = functools.reduce(
                    jnp.add, [Or[2 * s + half, pl.ds(h * TOK, TOK), :].astype(F32) for s in range(NX)])
                att[:, pl.ds((half * 4 + h) * HD, HD)] = o.astype(BF)

    wait_for(Gr.at[pl.ds(0, 15)], rsem.at[14])
    grad[...] = functools.reduce(jnp.add, [Gr[s].astype(F32) for s in range(16)])

    @pl.when(main)
    def _():
        wait_for(Kb.at[pl.ds(0, 7 * TOK), :], ssem.at[0])
        wait_for(Kb, ssem.at[16])
        wait_for(Kpos.at[pl.ds(0, 7)], ssem.at[1])
        wait_for(Kpos, ssem.at[17])
        wait_for(Or.at[pl.ds(0, 7)], ssem.at[2])
        wait_for(Kpos.at[pl.ds(0, 7)], ssem.at[3])
        wait_for(Or.at[pl.ds(0, 7)], ssem.at[6])
        wait_for(Vb.at[pl.ds(0, 7 * TOK), :], ssem.at[11])
        wait_for(Vb, ssem.at[18])
        wait_for(Ost.at[pl.ds(0, 3)], ssem.at[15])

    @pl.when(side)
    def _():
        wait_for(Ost, ssem.at[15])

    @pl.when(w_self)
    def _():
        wait_for(Ws.at[pl.ds(0, 3 * TOK), :], ssem.at[4])

    @pl.when(jnp.logical_not(w_self))
    def _():
        wait_for(Ws, ssem.at[4])

    wait_for(Hs.at[pl.ds(0, 7)], ssem.at[5])

    @pl.when(trace)
    def _():
        wait_for(ML.at[pl.ds(0, 3)], ssem.at[7])
        wait_for(Tsend, ssem.at[9])

    @pl.when(trace_owner)
    def _():
        wait_for(Tz.at[pl.ds(0, 3)], ssem.at[10])

    @pl.when(jnp.logical_and(trace, jnp.logical_not(trace_owner)))
    def _():
        wait_for(Tz, ssem.at[10])

    wait_for(Vr.at[pl.ds(0, 7)], ssem.at[8])

    @pl.when(owner)
    def _():
        wait_for(Vg.at[pl.ds(0, 7)], ssem.at[12])

    @pl.when(c == 1)
    def _():
        wait_for(Vg.at[pl.ds(0, 7)], ssem.at[13])

    wait_for(Gr.at[pl.ds(0, 15)], ssem.at[14])


def per_device(hidden_in, value_weight, queries, key_vectors, cotangent, doc_ids, positions):
    vmem = pl.BlockSpec(memory_space=pltpu.VMEM)
    anywhere = pl.BlockSpec(memory_space=pl.ANY)
    scratch = [
        pltpu.VMEM((8, TOK), jnp.int32),
        pltpu.VMEM((512, HD), BF),
        pltpu.VMEM((8, TOK, 512), BF),
        pltpu.VMEM((512, 1024), BF),
        pltpu.VMEM((1024, HD), BF),
        pltpu.VMEM((8, 8, TOK), jnp.int32),
        pltpu.VMEM((1024, TOK), F32),
        pltpu.VMEM((NX, TOK, 512), BF),
        pltpu.VMEM((NX, 8, TOK), jnp.int32),
        pltpu.VMEM((NX, TOK, 512), BF),
        pltpu.VMEM((TOK, 1024), BF),
        pltpu.VMEM((TOK, 1024), BF),
        pltpu.VMEM((1024, 256), F32),
        pltpu.VMEM((1024, 2048), BF),
        pltpu.VMEM((NX, NX, 8, 256), F32),
        pltpu.VMEM((NX, 8, 256), F32),
        pltpu.VMEM((2048, HD), BF),
        pltpu.VMEM((8, TOK, HD), BF),
        pltpu.VMEM((8, TOK, HD), BF),
        pltpu.VMEM((1024, HD), BF),
        pltpu.VMEM((HD, 1024), BF),
        pltpu.VMEM((512, HD), BF),
        pltpu.VMEM((512, HD), BF),
        pltpu.VMEM((4, TOK, HD), BF),
        pltpu.VMEM((8, TOK, HD), BF),
        pltpu.VMEM((8, TOK, HD), BF),
        pltpu.VMEM((NX, 512, HD), BF),
        pltpu.VMEM((2 * NX, 512, HD), BF),
        pltpu.VMEM((16, 32, HD), BF),
        pltpu.VMEM((16, 32, HD), BF),
        pltpu.SemaphoreType.DMA((19,)),
        pltpu.SemaphoreType.DMA((19,)),
        pltpu.SemaphoreType.DMA((6,)),
    ]
    return pl.pallas_call(
        kernel,
        name="trace_attention",
        out_shape=(
            jax.ShapeDtypeStruct((TOK, 1024), BF),
            jax.ShapeDtypeStruct((32, HD), F32),
        ),
        in_specs=[anywhere, vmem, anywhere, vmem, anywhere, vmem, vmem],
        out_specs=(vmem, vmem),
        scratch_shapes=scratch,
        compiler_params=pltpu.CompilerParams(
            collective_id=0, has_side_effects=True, vmem_limit_bytes=40 << 20
        ),
    )(
        hidden_in, value_weight, queries, key_vectors, cotangent,
        doc_ids.reshape(1, TOK), positions.reshape(1, TOK),
    )


def solution(mesh):
    in_specs = (
        P(("grp", "blk"), None),
        P("blk", "tp"),
        P(("grp", "blk"), "tp"),
        P(("grp", "blk"), "tp"),
        P(("grp", "blk"), "tp"),
        P(("grp", "blk")),
        P(("grp", "blk")),
    )
    out_specs = (P(("grp", "blk"), "tp"), P(("grp", "blk"), "tp"))
    return jax.shard_map(
        per_device, mesh=mesh, in_specs=in_specs, out_specs=out_specs, check_vma=False
    )
```

time: 1820 us -> 83.1 us (0.05)
  waiting for transfers between devices: 1550 us -> 0 us
  blocking collectives: 206 us -> 0 us
  Pallas kernels: 0 us -> 75.5 us
  matrix products: 23.4 us -> 0 us
    unnamed x6 -> x0, waiting for transfers between devices: 877 us -> none
    all_gather x3 -> x0, waiting for transfers between devices: 440 us -> none  [the longest x1 223 us: per_device(): lax.all_gather(values, 'blk', axis=0, tiled=True)]
    reduce_scatter x1 -> x0, waiting for transfers between devices: 236 us -> none  [per_device(): lax.psum_scatter(grad_head.astype(jnp.bfloat16), 'blk', scatter_dimension...]
    all_gather x2 -> x0, blocking collectives: 206 us -> none  [the longest x1 107 us: per_device(): lax.all_gather(doc_ids, 'blk', axis=0, tiled=True)]
    pallas_call x0 -> x1, Pallas kernels: none -> 75.5 us  [per_device(): pl.pallas_call(kernel, name='trace_attention', out_shape=(jax.ShapeDtypeS...]
    dot_general x8 -> x0, matrix products: 23.4 us -> none  [the longest x2 8.51 us: advance(): lax.dot_general(weights, c_blk, (((0,), (0,)), ((), ())), preferred_eleme...]
  transfers between devices with their start and end apart: 5 -> 0, of which waited for: 5 -> 0; matrix products, arithmetic and copies ran while one was open for 0% -> 0% of each run, Pallas kernels for 0% -> 0%
where the time goes in v1:
time: 83.1 us; the launch traced here: 82.8 us
  Pallas kernels  75.5 us (91%)
  local copies, waits for them, and re-layouts  6.6 us (8%)
    pallas_call x1, Pallas kernels, per_device(): pl.pallas_call(kernel, name='trace_attention', out_shape=(jax.ShapeDtypeS...  75.5 us
    unnamed x16, local copies, waits for them, and re-layouts  6.6 us

profile of v1, /device:TPU:1, one launch (start us, length us, event | category | flops | bytes accessed | tf_op | source)
XLA Modules:
  0.0 82.8 jit_solution(6761430459676298654)
XLA Ops:
  0.6 0.0 copy-start.5
  0.6 0.0 copy-start.6
  0.7 0.6 copy-done.5
  1.3 0.0 copy-done.6
  1.3 0.0 copy-start
  1.3 1.2 %copy-done = bf16[128,4096]{1,0:T(8,128)(2,1)S(1)} copy-done((bf16[128,4096]{1,0:T(8,128)(2,1)S(1)}, bf16[128,4096]{1,0:T(8,128)(2,1)}, u32[]{:S(2)}) %copy-start) | copy-done | bytes 1048600
  2.5 0.0 copy-start.1
  2.5 0.9 %copy-done.1 = bf16[128,1024]{1,0:T(8,128)(2,1)S(1)} copy-done((bf16[128,1024]{1,0:T(8,128)(2,1)S(1)}, bf16[128,1024]{1,0:T(8,128)(2,1)}, u32[]{:S(2)}) %copy-start.1) | copy-done | bytes 262168
  3.5 0.0 copy-start.2
  3.5 0.9 %copy-done.2 = bf16[128,1024]{1,0:T(8,128)(2,1)S(1)} copy-done((bf16[128,1024]{1,0:T(8,128)(2,1)S(1)}, bf16[128,1024]{1,0:T(8,128)(2,1)}, u32[]{:S(2)}) %copy-start.2) | copy-done | bytes 262168
  4.4 0.0 copy-start.3
  4.4 0.8 copy-done.3
  5.2 0.0 copy-start.4
  5.2 0.8 copy-done.4
  5.9 75.5 %trace_attention.1 = (bf16[128,1024]{1,0:T(8,128)(2,1)S(1)}, f32[32,128]{1,0:T(8,128)S(1)}) custom-call(bf16[128,4096]{1,0:T(8,128)(2,1)S(1)} %copy-done, bf16[128,128]{1,0:T(8,128)(2,1)S(1)} %copy-done.3, bf16[128,1024]{1,0:T(8,128)(2,1)S(1)} %copy-done.1, bf16[128,128]{1,0:T(8,128)(2,1)S(1)} %copy-done.4, bf16[128,1024]{1,0:T(8,128)(2,1)S(1)} %copy-done.2, ...), custom_call_target="tpu_custom_call" | custom-call | tf_op jit(solution)/shard_map/trace_attention/pallas_call | solution.py:478
  81.5 0.7 copy.11
  82.2 0.6 copy.12
Async XLA Ops:
  0.6 0.7 copy-start.5
  0.6 0.7 copy-start.6
  1.3 1.2 %copy-start = (bf16[128,4096]{1,0:T(8,128)(2,1)S(1)}, bf16[128,4096]{1,0:T(8,128)(2,1)}, u32[]{:S(2)}) copy-start(bf16[128,4096]{1,0:T(8,128)(2,1)} %hid.1) | copy-start | bytes 3145732
  2.5 0.9 %copy-start.1 = (bf16[128,1024]{1,0:T(8,128)(2,1)S(1)}, bf16[128,1024]{1,0:T(8,128)(2,1)}, u32[]{:S(2)}) copy-start(bf16[128,1024]{1,0:T(8,128)(2,1)} %qry.1) | copy-start | bytes 786436
  3.5 0.9 %copy-start.2 = (bf16[128,1024]{1,0:T(8,128)(2,1)S(1)}, bf16[128,1024]{1,0:T(8,128)(2,1)}, u32[]{:S(2)}) copy-start(bf16[128,1024]{1,0:T(8,128)(2,1)} %cot.1) | copy-start | bytes 786436
  4.4 0.8 copy-start.3
  5.2 0.8 copy-start.4

commit v2 on v1

v2 whole, which is shorter than its diff:
```python
import functools
import math

import jax
import jax.numpy as jnp
from jax import lax
from jax.experimental import pallas as pl
from jax.experimental.pallas import tpu as pltpu
from jax.sharding import PartitionSpec as P

HD = 128
NX = 4
NZ = 8
TOK = 128
SCALE = HD ** (-0.5) * math.log2(math.e)
HIDDEN = -1e30
MESH = pl.DeviceIdType.MESH
BF = jnp.bfloat16
F32 = jnp.float32
NT = (((1,), (1,)), ((), ()))


def wait_for(ref, sem):
    pltpu.make_async_copy(ref, ref, sem).wait()


def flip(row, rows):
    return jnp.transpose(jnp.broadcast_to(row, (rows, row.shape[1])))


def stack_pair(block):
    return jnp.concatenate([block[:, :HD], block[:, HD:]], axis=0)


def kernel(
    hid, wgt, qry, key, cot, doc, pos,
    att, grad,
    posv, docv, posb, Kv, Wg, Hf, Hs, HsT, Kx, KposT, Qb, Qpos, Cb, Qf, Cf, Sb, Pm, ML, Wr, Cs,
    Vp, Vs, Vb, VT, Tsend, Tsib, Tz, Tr, Vg, Ost, Or, Ah, Gst, Gr,
    ssem, rsem, lsem, far_in,
):
    grp = lax.axis_index("grp")
    blk = lax.axis_index("blk")
    tp = lax.axis_index("tp")
    zh, c = grp // 2, grp % 2
    x, z = blk // NZ, blk % NZ
    me = x * 2 + c
    z16 = zh * NZ + z
    trace = zh == 0
    main = jnp.logical_and(trace, c == 0)
    side = jnp.logical_and(trace, c == 1)
    local = jnp.logical_not(main)
    half_owner = z // 4 == c
    owner = jnp.where(trace, half_owner, c == 0)
    trace_owner = jnp.logical_and(trace, half_owner)

    def dev(x_, z_, zh_, c_):
        return (zh_ * 2 + c_, x_ * NZ + z_, tp)

    def put(src, dst, phase, to):
        pltpu.make_async_remote_copy(
            src_ref=src, dst_ref=dst, send_sem=ssem.at[phase], recv_sem=rsem.at[phase],
            device_id=to, device_id_type=MESH,
        ).start()

    near = []
    for k in (1, 2, 7, 6, 3, 5, 4):
        s = (me + k) % 8
        near.append((s // 2, s % 2))
    sib = dev(x, z, zh, 1 - c)
    line = [(z + k) % NZ for k in (4, 3, 5, 2, 6, 1, 7)]
    ring = [(x + k) % NX for k in (2, 1, 3)]
    half = pl.multiple_of(c * 512, 512)

    bar = pltpu.get_barrier_semaphore()

    def greet(to):
        pl.semaphore_signal(bar, inc=1, device_id=to, device_id_type=MESH)

    for xs, cs in near:
        greet(dev(xs, z, zh, cs))
    for zz in line:
        greet(dev(x, zz, zh, c))

    @pl.when(trace)
    def _():
        for zz in range(NZ):
            greet(dev(x, zz, 1, c))

    pltpu.make_async_copy(key, Kv.at[pl.ds(0, TOK), :], lsem.at[6]).start()
    pltpu.make_async_copy(pos, posv, lsem.at[7]).start()
    pltpu.make_async_copy(doc, docv, lsem.at[8]).start()
    for k in range(NX):
        pltpu.make_async_copy(
            hid.at[:, pl.ds(pl.multiple_of(k * 1024 + half, 512), 512)],
            Hf.at[c, :, pl.ds(k * 512, 512)], lsem.at[0]).start()
    for gi in range(2):
        pltpu.make_async_copy(
            hid.at[:, pl.ds(pl.multiple_of((c + 2 * gi) * 1024 + x * 256, 256), 256)],
            Hs.at[me, :, pl.ds(gi * 256, 256)], lsem.at[1]).start()

    @pl.when(main)
    def _():
        pltpu.make_async_copy(qry.at[:, pl.ds(0, 512)], Qb.at[x], lsem.at[2]).start()
        pltpu.make_async_copy(cot.at[:, pl.ds(0, 512)], Cb.at[x], lsem.at[3]).start()

    @pl.when(local)
    def _():
        pltpu.make_async_copy(qry, Qf, lsem.at[4]).start()
        pltpu.make_async_copy(cot, Cf, lsem.at[5]).start()

    wait_for(Kv.at[pl.ds(0, TOK), :], lsem.at[6])
    wait_for(posv, lsem.at[7])
    wait_for(docv, lsem.at[8])
    posb[...] = jnp.broadcast_to(posv[...], (8, TOK))
    p_row = posv[...].astype(F32)
    p_high = jnp.floor(p_row * (1.0 / 64.0))
    Kv[pl.ds(TOK, 16), :] = jnp.concatenate(
        [jnp.broadcast_to(p_high, (8, TOK)), jnp.broadcast_to(p_row - 64.0 * p_high, (8, TOK))],
        axis=0).astype(BF)

    @pl.when(main)
    def _():
        Kx[z] = Kv[...]
        Qpos[x] = posb[...]

    pl.semaphore_wait(bar, jnp.where(trace, 14, 22))

    @pl.when(main)
    def _():
        put(qry.at[:, pl.ds(512, 512)], Qb.at[x], 19, sib)
        for zz in line:
            put(Kv, Kx.at[z], 0, dev(x, zz, zh, 0))
        for xt in ring:
            put(qry.at[:, pl.ds(0, 512)], Qb.at[x], 2, dev(xt, z, zh, 0))
        for xs, cs in near:
            put(posb, Qpos.at[x], 3, dev(xs, z, zh, cs))
        put(cot.at[:, pl.ds(512, 512)], Cb.at[x], 20, sib)

    slot = pl.ds(pl.multiple_of((z % 4) * TOK, TOK), TOK)

    @pl.when(half_owner)
    def _():
        pltpu.make_async_copy(wgt, Wg.at[x, slot, :], rsem.at[4]).start()
        for zz in line:
            put(wgt, Wg.at[x, slot, :], 4, dev(x, zz, zh, c))

    @pl.when(main)
    def _():
        for xt in ring:
            put(cot.at[:, pl.ds(0, 512)], Cb.at[x], 6, dev(xt, z, zh, 0))

    for k in range(NX):
        put(hid.at[:, pl.ds(pl.multiple_of(k * 1024 + (1 - c) * 512, 512), 512)],
            Hf.at[c, :, pl.ds(k * 512, 512)], 21, sib)

    @pl.when(zh != 0)
    def _():
        for zz in range(NZ):
            pl.semaphore_signal(
                far_in, inc=1, device_id=dev(x, zz, 0, c), device_id_type=MESH)

    @pl.when(side)
    def _():
        wait_for(Qb.at[0], rsem.at[19])
        for xt in ring:
            put(Qb.at[x], Qb.at[x], 2, dev(xt, z, zh, 1))
        wait_for(Cb.at[0], rsem.at[20])
        for xt in ring:
            put(Cb.at[x], Cb.at[x], 6, dev(xt, z, zh, 1))

    @pl.when(main)
    def _():
        wait_for(Kx.at[pl.ds(0, 7)], rsem.at[0])
        put(Kx, Kx, 16, sib)

    wait_for(Wg.at[0], rsem.at[4])
    for xt in ring:
        put(Wg.at[x], Wg.at[x], 17, dev(xt, z, zh, c))

    @pl.when(trace)
    def _():
        @pl.when(c == 0)
        def _():
            wait_for(Qpos.at[pl.ds(0, 3)], rsem.at[3])
            wait_for(Qb.at[0], lsem.at[2])

        @pl.when(c == 1)
        def _():
            wait_for(Kx, rsem.at[16])
            wait_for(Qpos.at[pl.ds(0, 4)], rsem.at[3])

        wait_for(Qb.at[pl.ds(0, 3)], rsem.at[2])

        for t in range(NZ):
            digits = Kx[t, pl.ds(TOK, 16), :].astype(F32)
            KposT[pl.ds(t * TOK, TOK), :] = flip(digits[0:1] * 64.0 + digits[8:9], TOK)

        def score_block(xq, carry):
            q_at = Qpos[xq][0:1, :].astype(F32)
            tops, sums = [], []
            for pair in range(2):
                qp = stack_pair(Qb[xq, :, pl.ds(pair * 256, 256)])
                top = jnp.full((8, 256), HIDDEN, F32)
                for t in range(4):
                    rows = pl.ds(t * 256, 256)
                    kk = jnp.concatenate(
                        [Kx[2 * t, pl.ds(0, TOK), :], Kx[2 * t + 1, pl.ds(0, TOK), :]], axis=0)
                    s = lax.dot_general(kk, qp, NT, preferred_element_type=F32)
                    seen = KposT[rows, :] <= q_at
                    s = jnp.concatenate(
                        [jnp.where(seen, s[:, :HD], HIDDEN), jnp.where(seen, s[:, HD:], HIDDEN)],
                        axis=1)
                    Sb[rows, :] = s
                    top = jnp.maximum(top, jnp.max(s.reshape(32, 8, 256), axis=0))
                m = jnp.max(top, axis=0, keepdims=True) * SCALE
                total = jnp.zeros((8, 256), F32)
                at = pl.ds(pl.multiple_of(xq * 512 + pair * 256, 256), 256)
                for t in range(8):
                    rows = pl.ds(t * TOK, TOK)
                    p = jnp.exp2(Sb[rows, :] * SCALE - m)
                    total = total + jnp.sum(p.reshape(16, 8, 256), axis=0)
                    Pm[rows, at] = p.astype(BF)
                tops.append(m)
                sums.append(jnp.sum(total, axis=0, keepdims=True))
            ML[x, xq] = jnp.concatenate(
                tops + sums + [jnp.zeros((4, 256), F32)], axis=0)
            return carry

        lax.fori_loop(0, NX, score_block, 0)
        for xt in ring:
            put(ML.at[x], ML.at[x], 7, dev(xt, z, zh, c))

    for xs, cs in near:
        for gi in range(2):
            col = pl.multiple_of((cs + 2 * gi) * 1024 + xs * 256, 256)
            put(hid.at[:, pl.ds(col, 256)], Hs.at[me, :, pl.ds(gi * 256, 256)], 5,
                dev(xs, z, zh, cs))

    wait_for(Wg.at[pl.ds(0, 3)], rsem.at[17])
    wait_for(Hf.at[0], lsem.at[0])
    wait_for(Hf.at[0], rsem.at[21])
    w_all = Wg[...].reshape(2048, HD)
    Vp[...] = jnp.dot(Hf[1 - c], w_all, preferred_element_type=F32)
    put(Vp, Vs, 8, sib)
    own_part = jnp.dot(Hf[c], w_all, preferred_element_type=F32)
    wait_for(Vs, rsem.at[8])
    val = (own_part + Vs[...]).astype(BF)

    @pl.when(main)
    def _():
        rows = pl.ds(pl.multiple_of(z * TOK, TOK), TOK)
        Vb[rows, :] = val
        for zz in line:
            put(Vb.at[rows, :], Vb.at[rows, :], 11, dev(x, zz, zh, 0))

    @pl.when(trace)
    def _():
        @pl.when(c == 0)
        def _():
            wait_for(Cb.at[0], lsem.at[3])

        wait_for(Cb.at[pl.ds(0, 3)], rsem.at[6])
        wait_for(ML.at[pl.ds(0, 3)], rsem.at[7])

        def scale_block(xq, carry):
            parts = [ML[s, xq] for s in range(NX)]
            high = functools.reduce(jnp.maximum, [p[0:2] for p in parts])
            total = functools.reduce(
                jnp.add, [p[2:4] * jnp.exp2(p[0:2] - high) for p in parts])
            w = jnp.exp2(ML[x, xq][0:2] - high) / total
            Wr[xq] = jnp.concatenate([w, jnp.zeros((6, 256), F32)], axis=0)
            for pair in range(2):
                cp = stack_pair(Cb[xq, :, pl.ds(pair * 256, 256)]).astype(F32)
                rows = pl.ds(pl.multiple_of(xq * 512 + pair * 256, 256), 256)
                Cs[rows, :] = (cp * flip(w[pair:pair + 1], TOK)).astype(BF)
            return carry

        lax.fori_loop(0, NX, scale_block, 0)
        theirs = pl.ds(pl.multiple_of((1 - c) * 512, 512), 512)
        ours = pl.ds(half, 512)
        Tsend[...] = jnp.dot(Pm[theirs, :], Cs[...], preferred_element_type=F32).astype(BF)
        put(Tsend, Tsib, 9, sib)
        mine = jnp.dot(Pm[ours, :], Cs[...], preferred_element_type=F32)
        wait_for(Tsib, rsem.at[9])
        Tz[...] = (mine + Tsib[...].astype(F32)).astype(BF).reshape(4, TOK, HD)
        for k in range(4):
            zt = 4 * c + k

            @pl.when(zt != z)
            def _():
                put(Tz.at[k], Tr.at[z], 10, dev(x, zt, zh, c))

            @pl.when(zt == z)
            def _():
                Tr[z] = Tz[k]

    @pl.when(local)
    def _():
        wait_for(Qf, lsem.at[4])
        wait_for(Cf, lsem.at[5])
        val_t = jnp.transpose(val)
        d_row = docv[...].astype(F32)
        seen = jnp.logical_and(flip(p_row, TOK) <= p_row, flip(d_row, TOK) == d_row)
        terms = jnp.zeros((TOK, HD), F32)
        for pair in range(4):
            qp = stack_pair(Qf[:, pl.ds(pair * 256, 256)])
            s = lax.dot_general(Kv[pl.ds(0, TOK), :], qp, NT, preferred_element_type=F32)
            s = jnp.concatenate(
                [jnp.where(seen, s[:, :HD], HIDDEN), jnp.where(seen, s[:, HD:], HIDDEN)], axis=1)
            s = s * SCALE
            p = jnp.exp2(s - jnp.max(s, axis=0, keepdims=True))
            w = 1.0 / jnp.sum(p, axis=0, keepdims=True)
            pb = (p * w).astype(BF)
            o = jnp.dot(val_t, pb, preferred_element_type=F32)
            att[:, pl.ds(pair * 256, HD)] = jnp.transpose(o[:, :HD]).astype(BF)
            att[:, pl.ds(pair * 256 + HD, HD)] = jnp.transpose(o[:, HD:]).astype(BF)
            cp = stack_pair(Cf[:, pl.ds(pair * 256, 256)])
            terms = terms + jnp.dot(pb, cp, preferred_element_type=F32)
        Vg[me] = terms.astype(BF)
        for phase, core in ((12, 0), (13, 1)):
            @pl.when(c == core)
            def _():
                for xs, cs in near:
                    put(Vg.at[me], Vg.at[me], phase, dev(xs, z, zh, cs))

    wait_for(Hs.at[pl.ds(0, 7)], rsem.at[5])
    wait_for(Hs.at[0], lsem.at[1])
    for s in range(8):
        HsT[:, pl.ds(s * TOK, TOK)] = jnp.transpose(Hs[s])

    @pl.when(main)
    def _():
        wait_for(Vb.at[pl.ds(0, 7 * TOK), :], rsem.at[11])
        put(Vb, Vb, 18, sib)

    @pl.when(trace_owner)
    def _():
        wait_for(Tr.at[pl.ds(0, 7)], rsem.at[10])
        Vg[2 * x] = functools.reduce(
            jnp.add, [Tr[s].astype(F32) for s in range(NZ)]).astype(BF)
        for xs, cs in near:
            put(Vg.at[2 * x], Vg.at[2 * x], 12, dev(xs, z, zh, cs))

    @pl.when(trace)
    def _():
        @pl.when(c == 1)
        def _():
            wait_for(Vb, rsem.at[18])

        VT[...] = jnp.transpose(Vb[...])

        def out_block(xq, carry):
            w = Wr[xq]
            for pair in range(2):
                at = pl.ds(pl.multiple_of(xq * 512 + pair * 256, 256), 256)
                o = jnp.dot(VT[...], Pm[:, at], preferred_element_type=F32) * w[pair:pair + 1]
                Ost[xq, pl.ds(pair * 256, 256), :] = jnp.transpose(o).astype(BF)
            return carry

        lax.fori_loop(0, NX, out_block, 0)
        for xt in ring:
            put(Ost.at[xt], Or.at[x], 15, dev(xt, z, zh, c))
        Or[x] = Ost[x]

    for phase, sender in ((12, owner), (13, c == 1)):
        @pl.when(sender)
        def _():
            wait_for(Vg.at[pl.ds(0, 3)], rsem.at[phase])

        @pl.when(jnp.logical_not(sender))
        def _():
            wait_for(Vg.at[pl.ds(0, 4)], rsem.at[phase])

    vg_all = Vg[...].reshape(8 * TOK, HD)
    Gst[...] = jnp.dot(HsT[...], vg_all, preferred_element_type=F32).astype(BF).reshape(16, 32, HD)

    @pl.when(trace)
    def _():
        pl.semaphore_wait(far_in, NZ)

    for k in (8, 7, 9, 6, 10, 5, 11, 4, 12, 3, 13, 2, 14, 1, 15):
        zz = (z16 + k) % 16
        put(Gst.at[zz], Gr.at[z16], 14, dev(x, zz % NZ, zz // NZ, c))
    Gr[z16] = Gst[z16]

    @pl.when(trace)
    def _():
        wait_for(Or.at[pl.ds(0, 3)], rsem.at[15])
        for h in range(4):
            o = functools.reduce(
                jnp.add, [Or[s, pl.ds(h * TOK, TOK), :].astype(F32) for s in range(NX)])
            Ah[:, pl.ds(h * HD, HD)] = o.astype(BF)

        @pl.when(c == 1)
        def _():
            put(Ah, att.at[:, pl.ds(512, 512)], 22, sib)

        @pl.when(c == 0)
        def _():
            att[:, pl.ds(0, 512)] = Ah[...]
            wait_for(Ah, rsem.at[22])

    wait_for(Gr.at[pl.ds(0, 15)], rsem.at[14])
    grad[...] = functools.reduce(jnp.add, [Gr[s].astype(F32) for s in range(16)])

    @pl.when(main)
    def _():
        wait_for(Kx.at[pl.ds(0, 7)], ssem.at[0])
        wait_for(Kx, ssem.at[16])
        wait_for(Qpos, ssem.at[3])
        wait_for(Qb.at[0], ssem.at[19])
        wait_for(Cb.at[0], ssem.at[20])
        wait_for(Vb.at[pl.ds(0, 7 * TOK), :], ssem.at[11])
        wait_for(Vb, ssem.at[18])

    @pl.when(side)
    def _():
        wait_for(Ah, ssem.at[22])

    @pl.when(half_owner)
    def _():
        wait_for(Vg.at[pl.ds(0, 7)], ssem.at[4])

    wait_for(Wg.at[pl.ds(0, 3)], ssem.at[17])
    wait_for(Hf.at[0], ssem.at[21])
    wait_for(Hs.at[pl.ds(0, 7)], ssem.at[5])
    wait_for(Vp, ssem.at[8])

    @pl.when(trace)
    def _():
        wait_for(Qb.at[pl.ds(0, 3)], ssem.at[2])
        wait_for(Cb.at[pl.ds(0, 3)], ssem.at[6])
        wait_for(ML.at[pl.ds(0, 3)], ssem.at[7])
        wait_for(Tsend, ssem.at[9])
        wait_for(Or.at[pl.ds(0, 3)], ssem.at[15])

    @pl.when(trace_owner)
    def _():
        wait_for(Tz.at[pl.ds(0, 3)], ssem.at[10])

    @pl.when(jnp.logical_and(trace, jnp.logical_not(trace_owner)))
    def _():
        wait_for(Tz, ssem.at[10])

    @pl.when(owner)
    def _():
        wait_for(Vg.at[pl.ds(0, 7)], ssem.at[12])

    @pl.when(c == 1)
    def _():
        wait_for(Vg.at[pl.ds(0, 7)], ssem.at[13])

    wait_for(Gr.at[pl.ds(0, 15)], ssem.at[14])


def per_device(hidden_in, value_weight, queries, key_vectors, cotangent, doc_ids, positions):
    vmem = pl.BlockSpec(memory_space=pltpu.VMEM)
    hbm = pl.BlockSpec(memory_space=pltpu.HBM)
    scratch = [
        pltpu.VMEM((1, TOK), jnp.int32),
        pltpu.VMEM((1, TOK), jnp.int32),
        pltpu.VMEM((8, TOK), jnp.int32),
        pltpu.VMEM((TOK + 16, HD), BF),
        pltpu.VMEM((NX, 512, HD), BF),
        pltpu.VMEM((2, TOK, 2048), BF),
        pltpu.VMEM((8, TOK, 512), BF),
        pltpu.VMEM((512, 1024), BF),
        pltpu.VMEM((NZ, TOK + 16, HD), BF),
        pltpu.VMEM((1024, TOK), F32),
        pltpu.VMEM((NX, TOK, 512), BF),
        pltpu.VMEM((7, 8, TOK), jnp.int32),
        pltpu.VMEM((NX, TOK, 512), BF),
        pltpu.VMEM((TOK, 1024), BF),
        pltpu.VMEM((TOK, 1024), BF),
        pltpu.VMEM((1024, 256), F32),
        pltpu.VMEM((1024, 2048), BF),
        pltpu.VMEM((NX, NX, 8, 256), F32),
        pltpu.VMEM((NX, 8, 256), F32),
        pltpu.VMEM((2048, HD), BF),
        pltpu.VMEM((TOK, HD), F32),
        pltpu.VMEM((TOK, HD), F32),
        pltpu.VMEM((1024, HD), BF),
        pltpu.VMEM((HD, 1024), BF),
        pltpu.VMEM((512, HD), BF),
        pltpu.VMEM((512, HD), BF),
        pltpu.VMEM((4, TOK, HD), BF),
        pltpu.VMEM((8, TOK, HD), BF),
        pltpu.VMEM((8, TOK, HD), BF),
        pltpu.VMEM((NX, 512, HD), BF),
        pltpu.VMEM((NX, 512, HD), BF),
        pltpu.VMEM((TOK, 512), BF),
        pltpu.VMEM((16, 32, HD), BF),
        pltpu.VMEM((16, 32, HD), BF),
        pltpu.SemaphoreType.DMA((23,)),
        pltpu.SemaphoreType.DMA((23,)),
        pltpu.SemaphoreType.DMA((9,)),
        pltpu.SemaphoreType.REGULAR,
    ]
    return pl.pallas_call(
        kernel,
        name="trace_attention",
        out_shape=(
            jax.ShapeDtypeStruct((TOK, 1024), BF),
            jax.ShapeDtypeStruct((32, HD), F32),
        ),
        in_specs=[hbm] * 7,
        out_specs=(vmem, vmem),
        scratch_shapes=scratch,
        compiler_params=pltpu.CompilerParams(
            collective_id=0, has_side_effects=True, vmem_limit_bytes=56 << 20
        ),
    )(
        hidden_in, value_weight, queries, key_vectors, cotangent,
        doc_ids.reshape(1, TOK), positions.reshape(1, TOK),
    )


def solution(mesh):
    in_specs = (
        P(("grp", "blk"), None),
        P("blk", "tp"),
        P(("grp", "blk"), "tp"),
        P(("grp", "blk"), "tp"),
        P(("grp", "blk"), "tp"),
        P(("grp", "blk")),
        P(("grp", "blk")),
    )
    out_specs = (P(("grp", "blk"), "tp"), P(("grp", "blk"), "tp"))
    return jax.shard_map(
        per_device, mesh=mesh, in_specs=in_specs, out_specs=out_specs, check_vma=False
    )
```

time: 83.1 us -> 67.5 us (0.81)
  Pallas kernels: 75.5 us -> 64.1 us
  local copies, waits for them, and re-layouts: 6.6 us -> 2.28 us
    pallas_call x1, Pallas kernels: 75.5 us -> 64.1 us  [per_device(): pl.pallas_call(kernel, name='trace_attention', out_shape=(jax.ShapeDtypeS...]
    unnamed x16 -> x4, local copies, waits for them, and re-layouts: 6.6 us -> 2.28 us
where the time goes in v2:
time: 67.5 us; the launch traced here: 67 us
  Pallas kernels  64.1 us (95%)
  local copies, waits for them, and re-layouts  2.28 us (3%)
    pallas_call x1, Pallas kernels, per_device(): pl.pallas_call(kernel, name='trace_attention', out_shape=(jax.ShapeDtypeS...  64.1 us
    unnamed x4, local copies, waits for them, and re-layouts  2.28 us

profile of v2, /device:TPU:1, one launch (start us, length us, event | category | flops | bytes accessed | tf_op | source)
XLA Modules:
  0.0 67.0 jit_solution(4842111681302808223)
XLA Ops:
  0.6 64.1 %trace_attention.1 = (bf16[128,1024]{1,0:T(8,128)(2,1)}, f32[32,128]{1,0:T(8,128)}) custom-call(bf16[128,4096]{1,0:T(8,128)(2,1)} %hid.1, bf16[128,128]{1,0:T(8,128)(2,1)} %wgt.1, bf16[128,1024]{1,0:T(8,128)(2,1)} %qry.1, bf16[128,128]{1,0:T(8,128)(2,1)} %key.1, bf16[128,1024]{1,0:T(8,128)(2,1)} %cot.1, s32[1,128]{1,0:T(1,128)} %bitcast.2, s32[1,128]{1,0:T(1,128)} %bitcast.3), custom_call_target="tpu_custom_call" | custom-call | tf_op jit(solution)/shard_map/trace_attention/pallas_call | solution.py:500
  64.7 0.0 copy-start
  64.7 1.7 %copy.11 = bf16[128,1024]{1,0:T(8,128)(2,1)} copy(bf16[128,1024]{1,0:T(8,128)(2,1)} %get-tuple-element.4) | data formatting | bytes 524288
  66.4 0.0 copy-done
  66.4 0.6 copy.12
Async XLA Ops:
  64.7 1.7 %copy-start = (f32[32,128]{1,0:T(8,128)S(1)}, f32[32,128]{1,0:T(8,128)}, u32[]{:S(2)}) copy-start(f32[32,128]{1,0:T(8,128)} %get-tuple-element.5) | copy-start | bytes 49156

commit v3 on v2

--- a/solution.py
+++ b/solution.py
@@ -126,6 +126,14 @@
 
     pl.semaphore_wait(bar, jnp.where(trace, 14, 22))
 
+    slot = pl.ds(pl.multiple_of((z % 4) * TOK, TOK), TOK)
+
+    @pl.when(half_owner)
+    def _():
+        pltpu.make_async_copy(wgt, Wg.at[x, slot, :], rsem.at[4]).start()
+        for zz in line:
+            put(wgt, Wg.at[x, slot, :], 4, dev(x, zz, zh, c))
+
     @pl.when(main)
     def _():
         put(qry.at[:, pl.ds(512, 512)], Qb.at[x], 19, sib)
@@ -136,14 +144,6 @@
         for xs, cs in near:
             put(posb, Qpos.at[x], 3, dev(xs, z, zh, cs))
         put(cot.at[:, pl.ds(512, 512)], Cb.at[x], 20, sib)
-
-    slot = pl.ds(pl.multiple_of((z % 4) * TOK, TOK), TOK)
-
-    @pl.when(half_owner)
-    def _():
-        pltpu.make_async_copy(wgt, Wg.at[x, slot, :], rsem.at[4]).start()
-        for zz in line:
-            put(wgt, Wg.at[x, slot, :], 4, dev(x, zz, zh, c))
 
     @pl.when(main)
     def _():

time: 67.5 us -> 66.8 us (0.990)
  no operation moved by 1% of the time
where the time goes in v3:
time: 66.8 us; the launch traced here: 66.7 us
  Pallas kernels  63.7 us (95%)
  local copies, waits for them, and re-layouts  2.28 us (3%)
    pallas_call x1, Pallas kernels, per_device(): pl.pallas_call(kernel, name='trace_attention', out_shape=(jax.ShapeDtypeS...  63.7 us
    unnamed x4, local copies, waits for them, and re-layouts  2.28 us

profile of v3, /device:TPU:1, one launch (start us, length us, event | category | flops | bytes accessed | tf_op | source)
XLA Modules:
  0.0 66.7 jit_solution(3165104041383706652)
XLA Ops:
  0.6 63.7 %trace_attention.1 = (bf16[128,1024]{1,0:T(8,128)(2,1)}, f32[32,128]{1,0:T(8,128)}) custom-call(bf16[128,4096]{1,0:T(8,128)(2,1)} %hid.1, bf16[128,128]{1,0:T(8,128)(2,1)} %wgt.1, bf16[128,1024]{1,0:T(8,128)(2,1)} %qry.1, bf16[128,128]{1,0:T(8,128)(2,1)} %key.1, bf16[128,1024]{1,0:T(8,128)(2,1)} %cot.1, s32[1,128]{1,0:T(1,128)} %bitcast.2, s32[1,128]{1,0:T(1,128)} %bitcast.3), custom_call_target="tpu_custom_call" | custom-call | tf_op jit(solution)/shard_map/trace_attention/pallas_call | solution.py:500
  64.4 0.0 copy-start
  64.4 1.7 %copy.11 = bf16[128,1024]{1,0:T(8,128)(2,1)} copy(bf16[128,1024]{1,0:T(8,128)(2,1)} %get-tuple-element.4) | data formatting | bytes 524288
  66.1 0.0 copy-done
  66.1 0.6 copy.12
Async XLA Ops:
  64.4 1.7 %copy-start = (f32[32,128]{1,0:T(8,128)S(1)}, f32[32,128]{1,0:T(8,128)}, u32[]{:S(2)}) copy-start(f32[32,128]{1,0:T(8,128)} %get-tuple-element.5) | copy-start | bytes 49156

commit v4 on v3

--- a/solution.py
+++ b/solution.py
@@ -324,15 +324,15 @@
                 for xs, cs in near:
                     put(Vg.at[me], Vg.at[me], phase, dev(xs, z, zh, cs))
 
+    @pl.when(main)
+    def _():
+        wait_for(Vb.at[pl.ds(0, 7 * TOK), :], rsem.at[11])
+        put(Vb, Vb, 18, sib)
+
     wait_for(Hs.at[pl.ds(0, 7)], rsem.at[5])
     wait_for(Hs.at[0], lsem.at[1])
     for s in range(8):
         HsT[:, pl.ds(s * TOK, TOK)] = jnp.transpose(Hs[s])
-
-    @pl.when(main)
-    def _():
-        wait_for(Vb.at[pl.ds(0, 7 * TOK), :], rsem.at[11])
-        put(Vb, Vb, 18, sib)
 
     @pl.when(trace_owner)
     def _():

time: 66.8 us -> 66.4 us (level)
  no operation moved by 1% of the time
where the time goes in v4:
time: 66.4 us; the launch traced here: 66.2 us
  Pallas kernels  63.3 us (95%)
  local copies, waits for them, and re-layouts  2.28 us (3%)
    pallas_call x1, Pallas kernels, per_device(): pl.pallas_call(kernel, name='trace_attention', out_shape=(jax.ShapeDtypeS...  63.3 us
    unnamed x4, local copies, waits for them, and re-layouts  2.28 us

profile of v4, /device:TPU:1, one launch (start us, length us, event | category | flops | bytes accessed | tf_op | source)
XLA Modules:
  0.0 66.2 jit_solution(4159557289862596214)
XLA Ops:
  0.6 63.3 %trace_attention.1 = (bf16[128,1024]{1,0:T(8,128)(2,1)}, f32[32,128]{1,0:T(8,128)}) custom-call(bf16[128,4096]{1,0:T(8,128)(2,1)} %hid.1, bf16[128,128]{1,0:T(8,128)(2,1)} %wgt.1, bf16[128,1024]{1,0:T(8,128)(2,1)} %qry.1, bf16[128,128]{1,0:T(8,128)(2,1)} %key.1, bf16[128,1024]{1,0:T(8,128)(2,1)} %cot.1, s32[1,128]{1,0:T(1,128)} %bitcast.2, s32[1,128]{1,0:T(1,128)} %bitcast.3), custom_call_target="tpu_custom_call" | custom-call | tf_op jit(solution)/shard_map/trace_attention/pallas_call | solution.py:500
  63.9 0.0 copy-start
  63.9 1.7 %copy.11 = bf16[128,1024]{1,0:T(8,128)(2,1)} copy(bf16[128,1024]{1,0:T(8,128)(2,1)} %get-tuple-element.4) | data formatting | bytes 524288
  65.6 0.0 copy-done
  65.6 0.6 copy.12
Async XLA Ops:
  63.9 1.7 %copy-start = (f32[32,128]{1,0:T(8,128)S(1)}, f32[32,128]{1,0:T(8,128)}, u32[]{:S(2)}) copy-start(f32[32,128]{1,0:T(8,128)} %get-tuple-element.5) | copy-start | bytes 49156
